TPU v7x, 256 devices: a whole 4x4x8 slice. The times are simulated.
256 devices in a mesh: section: 16 (over x_hi, y, core), expert: 16 (over z, x_lo).
Axes of the slice: x: 4 (x_hi: 2, x_lo: 2; x = x_hi * 2 + x_lo), y: 4, z: 8, core: 2. Of those that a mesh axis runs over, the one named last changes fastest.
Arguments:
- forward_in: bfloat16 [16, 2048, 7168], P('section', 'expert'), may hold values from -6 to 6
- backward_saved: bfloat16 [16, 2048, 7168], P('section', 'expert'), may hold values from -6 to 6
- backward_grad: bfloat16 [16, 2048, 7168], P('section', 'expert'), may hold values from -6 to 6
- forward_routes: int32 [16, 2048, 2], P('section', 'expert'), may hold values from 0 to 127, as said below
- forward_gates: float32 [16, 2048, 2], P('section', 'expert'), may hold values from 0.2 to 1
- backward_routes: int32 [16, 2048, 2], P('section', 'expert'), may hold values from 0 to 127, as said below
- backward_gates: float32 [16, 2048, 2], P('section', 'expert'), may hold values from 0.2 to 1
- up_weight: bfloat16 [16, 7168, 2432], P('section', 'expert'), may hold values from -0.0625 to 0.0625
- down_weight: bfloat16 [16, 2432, 7168], P('section', None, 'expert'), may hold values from -0.125 to 0.125
Outputs:
- forward_out: bfloat16 [16, 2048, 7168], P('section', 'expert')
- backward_out: bfloat16 [16, 2048, 7168], P('section', 'expert')
Inputs may be any that keep to these rules, and one draw needn't show every extreme that they name: `forward_routes`: in every row the two ids differ. Of the 128 rows of one device (aligned blocks of a section), at most 17 name expert 0, and on some device exactly 17 do. `backward_routes`: in every row the two ids differ. Of the 128 rows of one device (aligned blocks of a section), at most 17 name expert 0, and on some device exactly 17 do.
All inputs are finite; a program needn't handle non-finite values.
Results may differ from a plain program's by a relative error of at most 0.005.
Values may be sent and summed in bfloat16 or wider, within the bound.
No kernel may reach another device: no remote copies, remote signals or barrier semaphores. Data moves between devices by JAX's collectives and lax.ppermute only.
A program may use at most 128 MiB of HBM per device.

v0:
```python
import jax
import jax.numpy as jnp
from jax import lax
from jax.sharding import PartitionSpec as P

MOST = 17


def shifted(value, axis, steps):
    count = lax.axis_size(axis)
    pairs = [(source, (source + steps) % count) for source in range(count)]
    return lax.ppermute(value, axis, pairs)


def window_pack(routes, gate_vals, capacity):
    hitting = routes == 0
    scaling = jnp.sum(jnp.where(hitting, gate_vals, jnp.zeros_like(gate_vals)), axis=1)
    routed = jnp.any(hitting, axis=1)
    slot_rows = jnp.nonzero(routed, size=capacity, fill_value=0)[0].astype(jnp.int32)
    live_count = jnp.sum(routed.astype(jnp.int32))
    slot_live = (jnp.arange(capacity, dtype=jnp.int32) < live_count).astype(jnp.float32)
    slot_gate = scaling[slot_rows] * slot_live
    return (slot_rows, slot_gate, slot_live)


def silu_slope(before):
    sigma = jax.nn.sigmoid(before)
    return sigma * (1.0 + before * (1.0 - sigma))


def times_transposed(left, right):
    return lax.dot_general(
        left, right, (((1,), (1,)), ((), ())), preferred_element_type=jnp.float32
    )


def per_device(
    forward_in,
    backward_saved,
    backward_grad,
    forward_routes,
    forward_gates,
    backward_routes,
    backward_gates,
    up_weight,
    down_weight,
):
    up_local = up_weight[0]
    down_local = down_weight[0]
    acts = forward_in[0]
    slot_rows, slot_gate, slot_live = window_pack(forward_routes[0], forward_gates[0], MOST)
    picked = acts[slot_rows]
    columns = lax.all_to_all(picked, "expert", split_axis=1, concat_axis=0, tiled=True)
    before = lax.psum(
        jnp.dot(columns, up_local, preferred_element_type=jnp.float32).astype(jnp.bfloat16),
        "expert",
    ).astype(jnp.float32)
    hidden = jax.nn.silu(before).astype(jnp.bfloat16)
    branch_cols = jnp.dot(hidden, down_local, preferred_element_type=jnp.float32).astype(
        jnp.bfloat16
    )
    branch = lax.all_to_all(branch_cols, "expert", split_axis=0, concat_axis=1, tiled=True)
    summed = (
        acts.astype(jnp.float32).at[slot_rows].add(slot_gate[:, None] * branch.astype(jnp.float32))
    )
    forward_out = shifted(summed.astype(jnp.bfloat16), "section", 1)
    saved = backward_saved[0]
    cotangent = backward_grad[0]
    back_rows, back_gate, back_live = window_pack(backward_routes[0], backward_gates[0], MOST)
    saved_picked = saved[back_rows]
    upstream = (back_gate[:, None] * cotangent[back_rows].astype(jnp.float32)).astype(jnp.bfloat16)
    saved_cols, upstream_cols = (
        lax.all_to_all(saved_picked, "expert", split_axis=1, concat_axis=0, tiled=True),
        lax.all_to_all(upstream, "expert", split_axis=1, concat_axis=0, tiled=True),
    )
    before_part = jnp.dot(saved_cols, up_local, preferred_element_type=jnp.float32)
    grad_part = jnp.dot(upstream_cols, down_local.T, preferred_element_type=jnp.float32)
    before_full, grad_full = (
        lax.psum(before_part.astype(jnp.bfloat16), "expert").astype(jnp.float32),
        lax.psum(grad_part.astype(jnp.bfloat16), "expert").astype(jnp.float32),
    )
    pre_grad = (grad_full * silu_slope(before_full)).astype(jnp.bfloat16)
    back_cols = times_transposed(pre_grad, up_local).astype(jnp.bfloat16)
    back = lax.all_to_all(back_cols, "expert", split_axis=0, concat_axis=1, tiled=True)
    grads = (
        cotangent.astype(jnp.float32)
        .at[back_rows]
        .add(back_live[:, None] * back.astype(jnp.float32))
    )
    backward_out = shifted(grads.astype(jnp.bfloat16), "section", -1)
    return (forward_out[None], backward_out[None])


def solution(mesh):
    return jax.shard_map(
        per_device,
        mesh=mesh,
        in_specs=(
            P("section", "expert", None),
            P("section", "expert", None),
            P("section", "expert", None),
            P("section", "expert", None),
            P("section", "expert", None),
            P("section", "expert", None),
            P("section", "expert", None),
            P("section", "expert", None),
            P("section", None, "expert"),
        ),
        out_specs=(P("section", "expert", None), P("section", "expert", None)),
        check_vma=False,
    )
```

profile of v0, /device:TPU:1, one launch (start us, length us, event | category | flops | bytes accessed | tf_op | source)
XLA Modules:
  0.0 371.9 jit_solution(13986920724362538084)
XLA Ops:
  7.2 0.8 fusion.48
  9.0 1.4 scatter_custom_fusion
  10.6 0.7 fusion.42
  11.8 2.7 gather_fusion.1
  14.9 0.9 copy.37
  15.8 10.0 %all-to-all-start = ((bf16[17,16,448]{2,0,1:T(8,128)(2,1)}), bf16[17,16,448]{2,0,1:T(8,128)(2,1)S(1)}, u32[]{:S(2)}, u32[]{:S(2)}) async-start(bf16[17,16,448]{2,0,1:T(8,128)(2,1)} %copy.37), calls=%async_computation | async-start | bytes 786432 | tf_op jit(solution)/shard_map/all_to_all | solution.py:53
  26.2 1.4 scatter_custom_fusion.2
  28.5 0.8 fusion.43
  29.3 0.7 gather_fusion.2
  30.0 2.7 gather_fusion.4
  33.0 0.9 copy.42
  33.9 2.7 gather_fusion.3
  36.9 2.2 all-to-all-done
  39.1 5.3 %all-to-all-start.3 = ((bf16[17,16,448]{2,0,1:T(8,128)(2,1)}), bf16[17,16,448]{2,0,1:T(8,128)(2,1)S(1)}, u32[]{:S(2)}, u32[]{:S(2)}) async-start(bf16[17,16,448]{2,0,1:T(8,128)(2,1)} %copy.42), calls=%async_computation.3 | async-start | bytes 786432 | tf_op jit(solution)/shard_map/all_to_all | solution.py:73
  45.2 0.9 copy.41
  46.1 10.6 %all-to-all-done.3 = bf16[17,16,448]{2,0,1:T(8,128)(2,1)S(1)} async-done(((bf16[17,16,448]{2,0,1:T(8,128)(2,1)}), bf16[17,16,448]{2,0,1:T(8,128)(2,1)S(1)}, u32[]{:S(2)}, u32[]{:S(2)}) %all-to-all-start.3) | async-done | bytes 243744 | tf_op jit(solution)/shard_map/all_to_all | solution.py:73
  56.7 4.1 %all-to-all-start.2 = ((bf16[17,16,448]{2,0,1:T(8,128)(2,1)}), bf16[17,16,448]{2,0,1:T(8,128)(2,1)S(1)}, u32[]{:S(2)}, u32[]{:S(2)}) async-start(bf16[17,16,448]{2,0,1:T(8,128)(2,1)} %copy.41), calls=%async_computation.2 | async-start | bytes 786432 | tf_op jit(solution)/shard_map/all_to_all | solution.py:74
  60.9 0.8 all_to_all.63
  61.9 10.1 %all-to-all-done.2 = bf16[17,16,448]{2,0,1:T(8,128)(2,1)S(1)} async-done(((bf16[17,16,448]{2,0,1:T(8,128)(2,1)}), bf16[17,16,448]{2,0,1:T(8,128)(2,1)S(1)}, u32[]{:S(2)}, u32[]{:S(2)}) %all-to-all-start.2) | async-done | bytes 243744 | tf_op jit(solution)/shard_map/all_to_all | solution.py:74
  72.1 2.0 convolution_convert_fusion
  74.1 2.0 convolution_convert_fusion.2
  76.1 2.0 convolution_convert_fusion.1
  78.7 0.7 gather_fusion
  79.4 1.2 compare_convert_fusion
  80.7 3.8 %bitcast_convert_fusion.1 = f32[128,7168]{1,0:T(8,128)} fusion(bf16[1,128,7168]{2,1,0:T(8,128)(2,1)} %param.9), kind=kLoop, calls=%fused_computation.85 | loop fusion | flops 917504 | bytes 5505024 | tf_op jit(solution)/shard_map/convert_element_type | solution.py:64
  84.5 2.2 bitcast_convert_fusion
  86.7 188.1 %all-reduce.3.cloned.1.call-done = (bf16[272,2432]{1,0:T(8,128)(2,1)}, bf16[272,2432]{1,0:T(8,128)(2,1)}, bf16[272,2432]{1,0:T(8,128)(2,1)}) async-done(((bf16[272,2432]{1,0:T(8,128)(2,1)}, bf16[272,2432]{1,0:T(8,128)(2,1)}, bf16[272,2432]{1,0:T(8,128)(2,1)}), (bf16[272,2432]{1,0:T(8,128)(2,1)}, bf16[272,2432]{1,0:T(8,128)(2,1)}, bf16[272,2432]{1,0:T(8,128)(2,1)})) %all-reduce.3.cloned.1.call-update) | async-done | bytes 3969040 | tf_op jit(solution)/shard_map/psum | solution.py:54
  274.7 2.9 fusion.25
  277.7 0.9 all_to_all.73
  278.5 5.5 %all-to-all-start.4 = ((bf16[16,17,448]{2,1,0:T(8,128)(2,1)}), bf16[16,17,448]{2,1,0:T(8,128)(2,1)S(1)}, u32[]{:S(2)}, u32[]{:S(2)}) async-start(bf16[16,17,448]{2,1,0:T(8,128)(2,1)} %all_to_all.73), calls=%async_computation.4 | async-start | bytes 786432 | tf_op jit(solution)/shard_map/all_to_all | solution.py:84
  284.0 2.9 fusion.20
  287.0 0.9 all_to_all.64
  287.8 9.6 %all-to-all-done.4 = bf16[16,17,448]{2,1,0:T(8,128)(2,1)S(1)} async-done(((bf16[16,17,448]{2,1,0:T(8,128)(2,1)}), bf16[16,17,448]{2,1,0:T(8,128)(2,1)S(1)}, u32[]{:S(2)}, u32[]{:S(2)}) %all-to-all-start.4) | async-done | bytes 243744 | tf_op jit(solution)/shard_map/all_to_all | solution.py:84
  297.4 4.2 %all-to-all-start.1 = ((bf16[16,17,448]{2,1,0:T(8,128)(2,1)}), bf16[16,17,448]{2,1,0:T(8,128)(2,1)}, u32[]{:S(2)}, u32[]{:S(2)}) async-start(bf16[16,17,448]{2,1,0:T(8,128)(2,1)} %all_to_all.64), calls=%async_computation.1 | async-start | bytes 786432 | tf_op jit(solution)/shard_map/all_to_all | solution.py:62
  301.7 1.1 compare_select_fusion.4
  303.4 10.4 %all-to-all-done.1 = bf16[16,17,448]{2,1,0:T(8,128)(2,1)} async-done(((bf16[16,17,448]{2,1,0:T(8,128)(2,1)}), bf16[16,17,448]{2,1,0:T(8,128)(2,1)}, u32[]{:S(2)}, u32[]{:S(2)}) %all-to-all-start.1) | async-done | bytes 243744 | tf_op jit(solution)/shard_map/all_to_all | solution.py:62
  313.9 1.1 convert_bitcast_fusion.1
  315.0 1.1 copy.38
  316.1 1.3 reshape.249
  317.4 5.2 %scatter_custom_fusion.1 = f32[128,7168]{1,0:T(8,128)} fusion(f32[128,7168]{1,0:T(8,128)} %bitcast_convert_fusion.1, s32[17]{0:T(128)} %copy-done.3, f32[17,7168]{1,0:T(8,128)S(1)} %reshape.249, f32[17]{0:T(128)} %compare_select_fusion.4), kind=kCustom, calls=%fused_computation.40 | custom fusion | flops 243712 | bytes 4157952 | tf_op jit(solution)/shard_map/scatter-add | solution.py:64
  322.6 3.5 convert_element_type.125
  326.1 4.7 %collective-permute-start = (bf16[128,7168]{1,0:T(8,128)(2,1)}, bf16[128,7168]{1,0:T(8,128)(2,1)}, u32[]{:S(2)}, u32[]{:S(2)}) collective-permute-start(bf16[128,7168]{1,0:T(8,128)(2,1)} %convert_element_type.125), channel_id=1, source_target_pairs={{0,16},{16,32},{32,48},{48,64},{64,80},{80,96},{96,112},{112,128},... | collective-permute-start | bytes 5505032 | tf_op jit(solution)/shard_map/ppermute | solution.py:12
  330.8 5.2 %scatter_custom_fusion.3 = f32[128,7168]{1,0:T(8,128)} fusion(f32[128,7168]{1,0:T(8,128)} %bitcast_convert_fusion, s32[17]{0:T(128)} %copy-done.4, f32[17,7168]{1,0:T(8,128)S(1)} %reshape.252, f32[17]{0:T(128)S(1)} %copy-done.9), kind=kCustom, calls=%fused_computation.38 | custom fusion | flops 243712 | bytes 4157508 | tf_op jit(solution)/shard_map/scatter-add | solution.py:88
  336.0 2.3 convert_element_type.143
  338.4 13.0 %collective-permute-done = bf16[128,7168]{1,0:T(8,128)(2,1)} collective-permute-done((bf16[128,7168]{1,0:T(8,128)(2,1)}, bf16[128,7168]{1,0:T(8,128)(2,1)}, u32[]{:S(2)}, u32[]{:S(2)}) %collective-permute-start) | collective-permute-done | bytes 1835040 | tf_op jit(solution)/shard_map/ppermute | solution.py:12
  351.3 9.7 %collective-permute-done.1 = bf16[128,7168]{1,0:T(8,128)(2,1)S(1)} collective-permute-done((bf16[128,7168]{1,0:T(8,128)(2,1)S(1)}, bf16[128,7168]{1,0:T(8,128)(2,1)S(1)}, u32[]{:S(2)}, u32[]{:S(2)}) %collective-permute-start.1) | collective-permute-done | bytes 1835040 | tf_op jit(solution)/shard_map/ppermute | solution.py:12
  361.0 2.8 copy.51
  363.8 1.2 copy.52
  (55 shorter events, 6.4 us)
Async XLA Ops:
  7.2 65.0 %copy-start = (bf16[1,448,2432]{2,1,0:T(8,128)(2,1)S(1)}, bf16[1,448,2432]{2,1,0:T(8,128)(2,1)}, u32[]{:S(2)}) copy-start(bf16[1,448,2432]{2,1,0:T(8,128)(2,1)} %param.16) | copy-start | bytes 6537220
  11.3 0.5 copy-start.3
  11.8 14.0 %copy-start.5 = (s32[1,128,2]{1,2,0:T(2,128)S(1)}, s32[1,128,2]{1,2,0:T(2,128)}, u32[]{:S(2)}) copy-start(s32[1,128,2]{1,2,0:T(2,128)} %param.14) | copy-start | bytes 3076
  11.8 17.4 %copy-start.6 = (f32[1,128,2]{1,2,0:T(2,128)S(1)}, f32[1,128,2]{1,2,0:T(2,128)}, u32[]{:S(2)}) copy-start(f32[1,128,2]{1,2,0:T(2,128)} %param.15) | copy-start | bytes 3076
  15.8 23.4 %all-to-all-start = ((bf16[17,16,448]{2,0,1:T(8,128)(2,1)}), bf16[17,16,448]{2,0,1:T(8,128)(2,1)S(1)}, u32[]{:S(2)}, u32[]{:S(2)}) async-start(bf16[17,16,448]{2,0,1:T(8,128)(2,1)} %copy.37), calls=%async_computation | async-start | bytes 786432 | tf_op jit(solution)/shard_map/all_to_all | solution.py:53
  29.2 4.7 %copy-start.4 = (s32[17]{0:T(128)}, s32[17]{0:T(128)S(1)}, u32[]{:S(2)}) copy-start(s32[17]{0:T(128)S(1)} %fusion.43) | copy-start | bytes 208
  39.1 17.6 %all-to-all-start.3 = ((bf16[17,16,448]{2,0,1:T(8,128)(2,1)}), bf16[17,16,448]{2,0,1:T(8,128)(2,1)S(1)}, u32[]{:S(2)}, u32[]{:S(2)}) async-start(bf16[17,16,448]{2,0,1:T(8,128)(2,1)} %copy.42), calls=%async_computation.3 | async-start | bytes 786432 | tf_op jit(solution)/shard_map/all_to_all | solution.py:73
  56.7 15.3 %all-to-all-start.2 = ((bf16[17,16,448]{2,0,1:T(8,128)(2,1)}), bf16[17,16,448]{2,0,1:T(8,128)(2,1)S(1)}, u32[]{:S(2)}, u32[]{:S(2)}) async-start(bf16[17,16,448]{2,0,1:T(8,128)(2,1)} %copy.41), calls=%async_computation.2 | async-start | bytes 786432 | tf_op jit(solution)/shard_map/all_to_all | solution.py:74
  60.9 213.9 %all-reduce.3.cloned.1.call-start = ((), (), s32[]{:S(2)}) async-start(), calls=%async_computation.5 | async-start | bytes 7938048 | tf_op jit(solution)/shard_map/psum | solution.py:54
  72.1 2.0 copy-start.2
  74.1 2.0 copy-start.10
  78.0 0.7 copy-start.7
  78.0 0.7 copy-start.8
  80.7 3.8 %copy-start.1 = (bf16[1,128,7168]{2,1,0:T(8,128)(2,1)S(1)}, bf16[1,128,7168]{2,1,0:T(8,128)(2,1)}, u32[]{:S(2)}) copy-start(bf16[1,128,7168]{2,1,0:T(8,128)(2,1)} %param.11) | copy-start | bytes 5505028
  278.5 18.9 %all-to-all-start.4 = ((bf16[16,17,448]{2,1,0:T(8,128)(2,1)}), bf16[16,17,448]{2,1,0:T(8,128)(2,1)S(1)}, u32[]{:S(2)}, u32[]{:S(2)}) async-start(bf16[16,17,448]{2,1,0:T(8,128)(2,1)} %all_to_all.73), calls=%async_computation.4 | async-start | bytes 786432 | tf_op jit(solution)/shard_map/all_to_all | solution.py:84
  297.4 16.4 %all-to-all-start.1 = ((bf16[16,17,448]{2,1,0:T(8,128)(2,1)}), bf16[16,17,448]{2,1,0:T(8,128)(2,1)}, u32[]{:S(2)}, u32[]{:S(2)}) async-start(bf16[16,17,448]{2,1,0:T(8,128)(2,1)} %all_to_all.64), calls=%async_computation.1 | async-start | bytes 786432 | tf_op jit(solution)/shard_map/all_to_all | solution.py:62
  322.6 8.2 %copy-start.9 = (f32[17]{0:T(128)S(1)}, f32[17]{0:T(128)}, u32[]{:S(2)}) copy-start(f32[17]{0:T(128)} %compare_convert_fusion) | copy-start | bytes 208
  326.1 25.2 %collective-permute-start = (bf16[128,7168]{1,0:T(8,128)(2,1)}, bf16[128,7168]{1,0:T(8,128)(2,1)}, u32[]{:S(2)}, u32[]{:S(2)}) collective-permute-start(bf16[128,7168]{1,0:T(8,128)(2,1)} %convert_element_type.125), channel_id=1, source_target_pairs={{0,16},{16,32},{32,48},{48,64},{64,80},{80,96},{96,112},{112,128},... | collective-permute-start | bytes 5505032 | tf_op jit(solution)/shard_map/ppermute | solution.py:12
  338.3 22.7 %collective-permute-start.1 = (bf16[128,7168]{1,0:T(8,128)(2,1)S(1)}, bf16[128,7168]{1,0:T(8,128)(2,1)S(1)}, u32[]{:S(2)}, u32[]{:S(2)}) collective-permute-start(bf16[128,7168]{1,0:T(8,128)(2,1)S(1)} %convert_element_type.143), channel_id=1, source_target_pairs={{0,240},{16,0},{32,16},{48,32},{64,48},{80,64},{96,80},{112,96},{1... | collective-permute-start | bytes 5505032 | tf_op jit(solution)/shard_map/ppermute | solution.py:12
Sparse Core Ops, SparseCore 0:
  78.2 196.5 all-reduce.2
where the time goes:
time: 375 us; the launch traced here: 372 us
  waiting for transfers between devices  254 us (68%)
  starting transfers between devices  34.1 us (9%)
  other arithmetic  33.4 us (9%)
  local copies, waits for them, and re-layouts  24.7 us (7%)
  between operations  14.3 us (4%)
  matrix products  11.7 us (3%)
    psum x1, waiting for transfers between devices, per_device(): lax.psum(jnp.dot(columns, up_local, preferred_element_type=jnp.float32).a...  188 us
    ppermute x2, waiting for transfers between devices, shifted(): return lax.ppermute(value, axis, pairs)  22.6 us
    all_to_all x1, waiting for transfers between devices, per_device(): lax.all_to_all(saved_picked, 'expert', split_axis=1, concat_axis=0, tiled...  10.6 us
    all_to_all x1, waiting for transfers between devices, per_device(): lax.all_to_all(branch_cols, 'expert', split_axis=0, concat_axis=1, tiled=...  10.4 us
    all_to_all x1, waiting for transfers between devices, per_device(): lax.all_to_all(upstream, 'expert', split_axis=1, concat_axis=0, tiled=True)  10.1 us
    all_to_all x1, starting transfers between devices, per_device(): lax.all_to_all(picked, 'expert', split_axis=1, concat_axis=0, tiled=True)  10 us
    all_to_all x1, waiting for transfers between devices, per_device(): lax.all_to_all(back_cols, 'expert', split_axis=0, concat_axis=1, tiled=True)  9.6 us
  transfers between devices with their start and end apart: 8, of which 8 were waited for; matrix products, arithmetic and copies ran while one was open for 9% of the time, Pallas kernels for 0%

commit v1 on v0

v1 whole, which is shorter than its diff:
```python
import functools

import jax
import jax.numpy as jnp
from jax import lax
from jax.experimental import pallas as pl
from jax.experimental.pallas import tpu as pltpu
from jax.sharding import PartitionSpec as P

MOST = 17
TOK = 128
D = 7168
FF = 2432
COLS = 448
NODES = 8
PICK = 56
CHUNK = 104
SENT = 72
BACK = 40
ROWS = 24
FIRST = 1280
BF = jnp.bfloat16
F32 = jnp.float32
VMEM_LIMIT = 48 * 1024 * 1024


def iota(shape, dim):
    return lax.broadcasted_iota(jnp.int32, shape, dim)


def dot(left, right):
    return jnp.dot(left, right, preferred_element_type=F32)


def dot_tn(left, right):
    return lax.dot_general(left, right, (((0,), (0,)), ((), ())), preferred_element_type=F32)


def dot_nt(left, right):
    return lax.dot_general(left, right, (((1,), (1,)), ((), ())), preferred_element_type=F32)


def onehot(cond):
    return jnp.where(cond, 1.0, 0.0).astype(BF)


def token_columns(routes, gates):
    hits = routes == 0
    hit = jnp.sum(jnp.where(hits, 1.0, 0.0), axis=1, keepdims=True)
    scaling = jnp.sum(jnp.where(hits, gates, 0.0), axis=1, keepdims=True)
    return hit, scaling


def across(column):
    wide = jnp.broadcast_to(column, (TOK, TOK)).astype(BF)
    eye = onehot(iota((TOK, TOK), 0) == iota((TOK, TOK), 1))
    return dot_tn(wide, eye)


def slot_rows(hit):
    wide = jnp.broadcast_to(hit, (TOK, TOK)).astype(BF)
    upto = onehot(iota((TOK, TOK), 0) <= iota((TOK, TOK), 1))
    rank = dot_tn(wide, upto)
    return jnp.where(across(hit) > 0.5, rank - 1.0, -1.0)


def placed(slots, rows, start):
    row = iota((rows, TOK), 0) - start
    return (slots[:rows] == row.astype(F32)) & (row >= 0)


def pick_kernel(froutes, fgates, broutes, bgates, acts, saved, cot, packed, kept, gate, meta, px, ps, pu, scale):
    @pl.when(pl.program_id(0) == 0)
    def _():
        fhit, fscaling = token_columns(froutes[...], fgates[...])
        bhit, bscaling = token_columns(broutes[...], bgates[...])
        fslots = slot_rows(fhit)
        bslots = slot_rows(bhit)
        px[...] = onehot(placed(fslots, PICK, 0))
        ps[...] = onehot(placed(bslots, PICK, MOST))
        pu[...] = onehot(placed(bslots, PICK, 2 * MOST))
        scale[...] = jnp.broadcast_to(bscaling, (TOK, TOK))
        hi = fscaling.astype(BF).astype(F32)
        mid = (fscaling - hi).astype(BF).astype(F32)
        low = fscaling - hi - mid
        frow = across(hi) + across(mid) + across(low)
        mine = jnp.sum(jnp.where(placed(fslots, ROWS, 0), frow[:ROWS], 0.0), axis=1, keepdims=True)
        gate[...] = jnp.broadcast_to(mine, (ROWS, TOK))
        meta[0] = fslots[:ROWS]
        meta[1] = bslots[:ROWS]

    x = acts[...]
    raw = cot[...]
    wide = jnp.concatenate([scale[...]] * 7, axis=1)
    upstream = (wide * raw.astype(F32)).astype(BF)
    fpart = dot(px[...], x)
    rows = fpart + dot(ps[...], saved[...]) + dot(pu[...], upstream)
    rows = rows.astype(BF)
    packed[0] = rows[:, :COLS]
    packed[1] = rows[:, COLS:]
    kept[0] = fpart.astype(BF)[:ROWS]
    here = iota((ROWS, PICK), 0)
    down = onehot((iota((ROWS, PICK), 1) == here + 2 * MOST) & (here < MOST))
    kept[1] = dot(down, dot(pu[...], raw).astype(BF)).astype(BF)


def pick(froutes, fgates, broutes, bgates, acts, saved, cot):
    width = 2 * COLS
    whole = lambda i: (0, 0)
    small = pl.BlockSpec((TOK, 2), whole)
    strip = pl.BlockSpec((TOK, width), lambda i: (0, i))
    return pl.pallas_call(
        pick_kernel,
        grid=(NODES,),
        out_shape=(
            jax.ShapeDtypeStruct((2 * NODES, PICK, COLS), BF),
            jax.ShapeDtypeStruct((2, ROWS, D), BF),
            jax.ShapeDtypeStruct((ROWS, TOK), F32),
            jax.ShapeDtypeStruct((2, ROWS, TOK), F32),
        ),
        in_specs=[small, small, small, small, strip, strip, strip],
        out_specs=(
            pl.BlockSpec((2, PICK, COLS), lambda i: (i, 0, 0)),
            pl.BlockSpec((2, ROWS, width), lambda i: (0, 0, i)),
            pl.BlockSpec((ROWS, TOK), whole),
            pl.BlockSpec((2, ROWS, TOK), lambda i: (0, 0, 0)),
        ),
        scratch_shapes=[
            pltpu.VMEM((PICK, TOK), BF),
            pltpu.VMEM((PICK, TOK), BF),
            pltpu.VMEM((PICK, TOK), BF),
            pltpu.VMEM((TOK, TOK), F32),
        ],
        compiler_params=pltpu.CompilerParams(vmem_limit_bytes=VMEM_LIMIT),
        name="pick",
    )(froutes, fgates, broutes, bgates, acts, saved, cot)


def spread(owner):
    r, c = iota((CHUNK, PICK), 0), iota((CHUNK, PICK), 1)
    out = None
    for start, source in ((0, MOST), (2 * MOST, 2 * MOST), (4 * MOST, 0)):
        j = r - start - owner * MOST
        here = (j >= 0) & (j < MOST) & (c == j + source)
        out = here if out is None else out | here
    return onehot(out)


def partial_kernel(node, picks, up, down, out, big):
    @pl.when(pl.program_id(0) == 0)
    def _():
        e0, e1 = spread(0), spread(1)
        for k in range(NODES):
            at = 2 * lax.rem(node[0] + k, NODES)
            both = dot(e0, picks[at]) + dot(e1, picks[at + 1])
            big[pl.ds(k * CHUNK, CHUNK), :] = both.astype(BF)

    rows = big[...]
    ups = dot(rows, up[...]).astype(BF)
    downs = dot_nt(rows, down[...]).astype(BF)
    for k in range(NODES):
        r = iota((CHUNK, ups.shape[1]), 0)
        mine = slice(k * CHUNK, (k + 1) * CHUNK)
        out[k] = jnp.where((r >= 2 * MOST) & (r < 4 * MOST), downs[mine], ups[mine])


def partial_sums(node, picks, up, down):
    width = 256
    return pl.pallas_call(
        partial_kernel,
        grid=(pl.cdiv(FF, width),),
        out_shape=jax.ShapeDtypeStruct((NODES, CHUNK, FF), BF),
        in_specs=[
            pl.BlockSpec(memory_space=pltpu.SMEM),
            pl.BlockSpec((2 * NODES, PICK, COLS), lambda i: (0, 0, 0)),
            pl.BlockSpec((COLS, width), lambda i: (0, i)),
            pl.BlockSpec((width, COLS), lambda i: (i, 0)),
        ],
        out_specs=pl.BlockSpec((NODES, CHUNK, width), lambda i: (0, 0, i)),
        scratch_shapes=[pltpu.VMEM((NODES * CHUNK, COLS), BF)],
        compiler_params=pltpu.CompilerParams(vmem_limit_bytes=VMEM_LIMIT),
        name="partials",
    )(node, picks, up, down)


def gather_rows(owner, start):
    r, c = iota((BACK, SENT), 0), iota((BACK, SENT), 1)
    j = r - start
    return onehot((j >= 0) & (j < MOST) & (c == j + 2 * start + owner * MOST))


def outward_kernel(node, up, down, *refs):
    *parts, out, first, second = refs
    space = 80
    for k in range(NODES):
        if k == 4:
            pieces = parts[8:12]
            for held, head, tail in ((first, pieces[0], pieces[1]), (second, pieces[2], pieces[3])):
                held[pl.ds(k * space, 32), :] = head[...]
                held[pl.ds(k * space + 32, SENT - 32), :] = tail[...]
        else:
            at = 2 * k if k < 4 else 2 * k + 2
            first[pl.ds(k * space, SENT), :] = parts[at][...]
            second[pl.ds(k * space, SENT), :] = parts[at + 1][...]
    branch = (dot(first[...], down[:FIRST, :]) + dot(second[...], down[FIRST:, :])).astype(BF)
    back = (dot_nt(first[...], up[:, :FIRST]) + dot_nt(second[...], up[:, FIRST:])).astype(BF)
    for k in range(NODES):
        mine = slice(k * space, k * space + SENT)
        at = 2 * lax.rem(node[0] + NODES - k, NODES)
        for owner in range(2):
            rows = dot(gather_rows(owner, 0), branch[mine]) + dot(gather_rows(owner, MOST), back[mine])
            out[at + owner] = rows.astype(BF)


def outward(node, up, down, parts):
    vmem = pl.BlockSpec(memory_space=pltpu.VMEM)
    return pl.pallas_call(
        outward_kernel,
        out_shape=jax.ShapeDtypeStruct((2 * NODES, BACK, COLS), BF),
        in_specs=[pl.BlockSpec(memory_space=pltpu.SMEM)] + [vmem] * (2 + len(parts)),
        out_specs=vmem,
        scratch_shapes=[pltpu.VMEM((NODES * 80, FIRST), BF), pltpu.VMEM((NODES * 80, FF - FIRST), BF)],
        compiler_params=pltpu.CompilerParams(vmem_limit_bytes=VMEM_LIMIT),
        name="outward",
    )(node, up, down, *parts)


def row_kernel(back, kept, gate, meta, fout, bout):
    both = jnp.concatenate([back[0], back[1]], axis=1)
    r, c = iota((ROWS, BACK), 0), iota((ROWS, BACK), 1)
    branch = dot(onehot((r < MOST) & (c == r)), both)
    grads = dot(onehot((r < MOST) & (c == r + MOST)), both)
    wide = jnp.concatenate([gate[...]] * 7, axis=1)
    fmeta = jnp.concatenate([meta[0]] * 7, axis=1)
    bmeta = jnp.concatenate([meta[1]] * 7, axis=1)
    live = iota(wide.shape, 0) < MOST
    fout[...] = jnp.where(live, kept[0].astype(F32) + wide * branch, fmeta).astype(BF)
    bout[...] = jnp.where(live, kept[1].astype(F32) + grads, bmeta).astype(BF)


def new_rows(back, kept, gate, meta):
    width = 2 * COLS
    return pl.pallas_call(
        row_kernel,
        grid=(NODES,),
        out_shape=(jax.ShapeDtypeStruct((ROWS, D), BF),) * 2,
        in_specs=[
            pl.BlockSpec((2, BACK, COLS), lambda i: (i, 0, 0)),
            pl.BlockSpec((2, ROWS, width), lambda i: (0, 0, i)),
            pl.BlockSpec((ROWS, TOK), lambda i: (0, 0)),
            pl.BlockSpec((2, ROWS, TOK), lambda i: (0, 0, 0)),
        ],
        out_specs=(pl.BlockSpec((ROWS, width), lambda i: (0, i)),) * 2,
        compiler_params=pltpu.CompilerParams(vmem_limit_bytes=VMEM_LIMIT),
        name="new_rows",
    )(back, kept, gate, meta)


def patch_kernel(fraw, frows, fhead, braw, brows, bhead, fout, bout):
    for raw, rows, head, out in ((fraw, frows, fhead, fout), (braw, brows, bhead, bout)):
        line = iota((ROWS, TOK), 0)
        slots = jnp.sum(jnp.where(line == MOST, head[...].astype(F32), 0.0), axis=0, keepdims=True)
        chosen = onehot((slots == line.astype(F32)) & (line < MOST))
        fresh = dot_tn(chosen, rows[...])
        mask = dot_tn(chosen, jnp.ones((ROWS, TOK), BF))
        mask = jnp.concatenate([mask] * (out.shape[1] // TOK), axis=1)
        out[...] = jnp.where(mask > 0.5, fresh, raw[...].astype(F32)).astype(BF)


def patch(fraw, frows, braw, brows):
    width = 1024
    strip = pl.BlockSpec((TOK, width), lambda i: (0, i))
    rows = pl.BlockSpec((ROWS, width), lambda i: (0, i))
    head = pl.BlockSpec((ROWS, TOK), lambda i: (0, 0))
    return pl.pallas_call(
        patch_kernel,
        grid=(D // width,),
        out_shape=(jax.ShapeDtypeStruct((TOK, D), BF),) * 2,
        in_specs=[strip, rows, head, strip, rows, head],
        out_specs=(strip, strip),
        compiler_params=pltpu.CompilerParams(vmem_limit_bytes=VMEM_LIMIT),
        name="patch",
    )(fraw, frows, frows, braw, brows, brows)


def around(value, steps):
    pairs = [(2 * z + x, 2 * ((z + steps) % NODES) + x) for z in range(NODES) for x in range(2)]
    return lax.ppermute(value, "expert", pairs)


def across_x(value):
    return lax.ppermute(value, "expert", [(e, e ^ 1) for e in range(2 * NODES)])


def section_shift(value, steps):
    count = lax.axis_size("section")
    return lax.ppermute(value, "section", [(s, (s + steps) % count) for s in range(count)])


def add(*terms):
    return functools.reduce(lambda a, b: a + b, [t.astype(F32) for t in terms]).astype(BF)


def scatter_ring(part):
    half = 48
    right = around(part[4, :half], 1)
    left = around(part[4, half:], -1)
    right = jnp.concatenate([add(part[3, :half], right), part[3, half:]])
    left = jnp.concatenate([part[5, :half], add(part[5, half:], left)])
    for k in (2, 1):
        right = add(part[k], around(right, 1))
        left = add(part[NODES - k], around(left, -1))
    total = add(part[0], around(right, 1), around(left, -1))
    return total.astype(F32) + across_x(total).astype(F32)


def activate(total):
    before = total[: 2 * MOST]
    grad = total[2 * MOST : 4 * MOST]
    hidden = jax.nn.silu(total[4 * MOST : 6 * MOST])
    sigma = jax.nn.sigmoid(before)
    pre_grad = grad * (sigma * (1.0 + before * (1.0 - sigma)))
    pad = jnp.zeros((SENT - 4 * MOST, total.shape[1]), F32)
    return jnp.concatenate([hidden, pre_grad, pad]).astype(BF)


def gather_ring(mine):
    ups, downs = [mine], [mine]
    for _ in range(3):
        ups.append(around(ups[-1], 1))
        downs.append(around(downs[-1], -1))
    head = around(ups[-1][:32], 1)
    tail = around(downs[-1][32:], -1)
    return ups[:4], (head, tail), downs[:0:-1]


def per_device(
    forward_in,
    backward_saved,
    backward_grad,
    forward_routes,
    forward_gates,
    backward_routes,
    backward_gates,
    up_weight,
    down_weight,
):
    up, down = up_weight[0], down_weight[0]
    node = (lax.axis_index("expert") // 2).astype(jnp.int32)[None]
    fraw = section_shift(forward_in[0], 1)
    braw = section_shift(backward_grad[0], -1)
    packed, kept, gate, meta = pick(
        forward_routes[0],
        forward_gates[0],
        backward_routes[0],
        backward_gates[0],
        forward_in[0],
        backward_saved[0],
        backward_grad[0],
    )
    picks = lax.all_to_all(packed, "expert", split_axis=0, concat_axis=0, tiled=True)
    part = partial_sums(node, picks, up, down)
    streams = []
    for cols in (slice(0, FIRST), slice(FIRST, FF)):
        streams.append(gather_ring(activate(scatter_ring(part[:, :, cols]))))
    (ups1, mid1, downs1), (ups2, mid2, downs2) = streams
    parts = []
    for one, two in zip(ups1, ups2):
        parts += [one, two]
    parts += [*mid1, *mid2]
    for one, two in zip(downs1, downs2):
        parts += [one, two]
    out = outward(node, up, down, parts)
    back = lax.all_to_all(out, "expert", split_axis=0, concat_axis=0, tiled=True)
    frows, brows = new_rows(back, kept, gate, meta)
    forward_out, backward_out = patch(
        fraw, section_shift(frows, 1), braw, section_shift(brows, -1)
    )
    return forward_out[None], backward_out[None]


def solution(mesh):
    row = P("section", "expert", None)
    return jax.shard_map(
        per_device,
        mesh=mesh,
        in_specs=(row, row, row, row, row, row, row, row, P("section", None, "expert")),
        out_specs=(row, row),
        check_vma=False,
    )
```

time: 375 us -> 209 us (0.56)
  waiting for transfers between devices: 254 us -> 61.4 us
  starting transfers between devices: 34.1 us -> 72 us
  other arithmetic: 33.4 us -> 4.27 us
  Pallas kernels: 0 us -> 28.2 us
  blocking collectives: 0 us -> 21.9 us
  between operations: 14.3 us -> 0.99 us
  matrix products: 11.7 us -> 0 us
  local copies, waits for them, and re-layouts: 24.7 us -> 16.2 us
    psum x1 -> x0, waiting for transfers between devices: 188 us -> none  [per_device(): lax.psum(jnp.dot(columns, up_local, preferred_element_type=jnp.float32).a...]
    ppermute x2 -> x38, starting transfers between devices: 4.79 us -> 61.9 us  [the longest x32 39.9 us: around(): return lax.ppermute(value, 'expert', pairs)]
    pallas_call x0 -> x5, Pallas kernels: none -> 28.2 us  [the longest x1 8.59 us: partial_sums(): pl.pallas_call(partial_kernel, grid=(pl.cdiv(FF, width),), out_shape=jax....]
    all_to_all x5 -> x1, waiting for transfers between devices: 43 us -> 19.6 us  [per_device(): lax.all_to_all(packed, 'expert', split_axis=0, concat_axis=0, tiled=True)]
    all_to_all x0 -> x1, blocking collectives: none -> 21.9 us  [per_device(): lax.all_to_all(out, 'expert', split_axis=0, concat_axis=0, tiled=True)]
    all_to_all x5 -> x1, starting transfers between devices: 29.2 us -> 10 us  [per_device(): lax.all_to_all(packed, 'expert', split_axis=0, concat_axis=0, tiled=True)]
    ppermute x2 -> x38, waiting for transfers between devices: 22.6 us -> 41.8 us  [the longest x32 31.7 us: around(): return lax.ppermute(value, 'expert', pairs)]
    scatter-add x4 -> x0, other arithmetic: 13.2 us -> none  [the longest x1 5.21 us: per_device(): acts.astype(jnp.float32).at[slot_rows]]
  transfers between devices with their start and end apart: 8 -> 39, of which waited for: 8 -> 16; matrix products, arithmetic and copies ran while one was open for 9% -> 4% of each run, Pallas kernels for 0% -> 4%
where the time goes in v1:
time: 209 us; the launch traced here: 205 us
  starting transfers between devices  72 us (34%)
  waiting for transfers between devices  61.4 us (29%)
  Pallas kernels  28.2 us (13%)
  blocking collectives  21.9 us (10%)
  local copies, waits for them, and re-layouts  16.2 us (8%)
  other arithmetic  4.27 us (2%)
    ppermute x32, starting transfers between devices, around(): return lax.ppermute(value, 'expert', pairs)  39.9 us
    ppermute x32, waiting for transfers between devices, around(): return lax.ppermute(value, 'expert', pairs)  31.7 us
    all_to_all x1, blocking collectives, per_device(): lax.all_to_all(out, 'expert', split_axis=0, concat_axis=0, tiled=True)  21.9 us
    ppermute x4, starting transfers between devices, section_shift(): lax.ppermute(value, 'section', [(s, (s + steps) % count) for s in range(c...  20.6 us
    all_to_all x1, waiting for transfers between devices, per_device(): lax.all_to_all(packed, 'expert', split_axis=0, concat_axis=0, tiled=True)  19.6 us
    unnamed x25, local copies, waits for them, and re-layouts  11.8 us
    all_to_all x1, starting transfers between devices, per_device(): lax.all_to_all(packed, 'expert', split_axis=0, concat_axis=0, tiled=True)  10 us
    pallas_call x1, Pallas kernels, partial_sums(): pl.pallas_call(partial_kernel, grid=(pl.cdiv(FF, width),), out_shape=jax....  8.59 us
  transfers between devices with their start and end apart: 39, of which 16 were waited for; matrix products, arithmetic and copies ran while one was open for 4% of the time, Pallas kernels for 4%

profile of v1, /device:TPU:1, one launch (start us, length us, event | category | flops | bytes accessed | tf_op | source)
XLA Modules:
  0.0 205.0 jit_solution(10309935516634153522)
XLA Ops:
  3.8 1.5 copy-done.3
  5.3 1.5 copy-done.4
  6.8 7.3 %pick.1 = (bf16[16,56,448]{2,1,0:T(8,128)(2,1)}, bf16[2,24,7168]{2,1,0:T(8,128)(2,1)S(1)}, f32[24,128]{1,0:T(8,128)S(1)}, f32[2,24,128]{2,1,0:T(8,128)S(1)}) custom-call(s32[128,2]{1,0:T(8,128)S(1)} %bitcast.105, f32[128,2]{1,0:T(8,128)S(1)} %bitcast.106, s32[128,2]{1,0:T(8,128)S(1)} %bitcast.107, f32[128,2]{1,0:T(8,128)S(1)} %bitcast.108, ...), custom_call_target="tpu_custom_call" | custom-call | tf_op jit(solution)/shard_map/pick/pallas_call | solution.py:112
  14.9 10.0 %all-to-all-start = ((bf16[16,56,448]{2,1,0:T(8,128)(2,1)}), bf16[16,56,448]{2,1,0:T(8,128)(2,1)S(1)}, u32[]{:S(2)}, u32[]{:S(2)}) async-start(bf16[16,56,448]{2,1,0:T(8,128)(2,1)} %get-tuple-element.10), calls=%async_computation | async-start | bytes 1835008 | tf_op jit(solution)/shard_map/all_to_all | solution.py:361
  24.9 3.2 %copy.11 = bf16[1,2432,448]{2,1,0:T(8,128)(2,1)S(1)} copy(bf16[1,2432,448]{1,2,0:T(8,128)(2,1)} %param.17) | data formatting | bytes 4358144 | tf_op args[8]
  28.2 19.6 %all-to-all-done.picks = bf16[16,56,448]{2,1,0:T(8,128)(2,1)S(1)} async-done(((bf16[16,56,448]{2,1,0:T(8,128)(2,1)}), bf16[16,56,448]{2,1,0:T(8,128)(2,1)S(1)}, u32[]{:S(2)}, u32[]{:S(2)}) %all-to-all-start) | async-done | bytes 802848 | tf_op jit(solution)/shard_map/all_to_all | solution.py:361
  47.9 1.6 copy-done.1
  49.5 8.6 %partials.1 = bf16[8,104,2432]{2,1,0:T(8,128)(2,1)} custom-call(s32[1]{0:T(128)} %bitcast.1.node, bf16[16,56,448]{2,1,0:T(8,128)(2,1)S(1)} %all-to-all-done.picks, bf16[448,2432]{1,0:T(8,128)(2,1)S(1)} %bitcast.100, bf16[2432,448]{1,0:T(8,128)(2,1)S(1)} %bitcast.98), custom_call_target="tpu_custom_call" | custom-call | tf_op jit(solution)/shard_map/partials/pallas_call | solution.py:169
  58.1 1.1 slice_bitcast_fusion.15
  59.2 1.2 slice_bitcast_fusion.20
  60.4 1.0 slice_bitcast_fusion.12
  63.2 2.0 collective-permute-start.14
  67.7 1.2 collective-permute-start.11
  68.9 2.9 %collective-permute-done.1 = bf16[48,1280]{1,0:T(8,128)(2,1)S(1)} collective-permute-done((bf16[48,1280]{1,0:T(8,128)(2,1)S(1)}, bf16[48,1280]{1,0:T(8,128)(2,1)S(1)}, u32[]{:S(2)}, u32[]{:S(2)}) %collective-permute-start.1) | collective-permute-done | bytes 122912 | tf_op jit(solution)/shard_map/ppermute | solution.py:288
  73.8 2.7 %collective-permute-start.15 = (bf16[104,1152]{1,0:T(8,128)(2,1)S(1)}, bf16[104,1152]{1,0:T(8,128)(2,1)S(1)}, u32[]{:S(2)}, u32[]{:S(2)}) collective-permute-start(bf16[104,1152]{1,0:T(8,128)(2,1)S(1)} %pad_maximum_fusion.3), channel_id=1, source_target_pairs={{0,14},{1,15},{2,0},{3,1},{4,2},{5,3},{6,4},{7,5},{8,6},{9,7},{10,... | collective-permute-start | bytes 718856 | tf_op jit(solution)/shard_map/ppermute | solution.py:288
  76.8 1.5 collective-permute-start.12
  78.3 3.3 %collective-permute-done.2 = bf16[104,1280]{1,0:T(8,128)(2,1)S(1)} collective-permute-done((bf16[104,1280]{1,0:T(8,128)(2,1)S(1)}, bf16[104,1280]{1,0:T(8,128)(2,1)S(1)}, u32[]{:S(2)}, u32[]{:S(2)}) %collective-permute-start.2) | collective-permute-done | bytes 266272 | tf_op jit(solution)/shard_map/ppermute | solution.py:288
  81.7 5.0 %collective-permute-done.12 = bf16[104,1152]{1,0:T(8,128)(2,1)S(1)} collective-permute-done((bf16[104,1152]{1,0:T(8,128)(2,1)S(1)}, bf16[104,1152]{1,0:T(8,128)(2,1)S(1)}, u32[]{:S(2)}, u32[]{:S(2)}) %collective-permute-start.12) | collective-permute-done | bytes 239648 | tf_op jit(solution)/shard_map/ppermute | solution.py:288
  86.9 1.5 collective-permute-start.13
  88.4 4.0 %collective-permute-done.3 = bf16[104,1280]{1,0:T(8,128)(2,1)S(1)} collective-permute-done((bf16[104,1280]{1,0:T(8,128)(2,1)S(1)}, bf16[104,1280]{1,0:T(8,128)(2,1)S(1)}, u32[]{:S(2)}, u32[]{:S(2)}) %collective-permute-start.3) | collective-permute-done | bytes 266272 | tf_op jit(solution)/shard_map/ppermute | solution.py:288
  92.7 1.5 collective-permute-start.4
  94.2 1.4 collective-permute-start.17
  95.6 3.5 %collective-permute-done.7 = bf16[104,1280]{1,0:T(8,128)(2,1)S(1)} collective-permute-done((bf16[104,1280]{1,0:T(8,128)(2,1)S(1)}, bf16[104,1280]{1,0:T(8,128)(2,1)S(1)}, u32[]{:S(2)}, u32[]{:S(2)}) %collective-permute-start.7) | collective-permute-done | bytes 266272 | tf_op jit(solution)/shard_map/ppermute | solution.py:288
  99.2 1.6 collective-permute-start.8
  100.7 2.9 %collective-permute-done.17 = bf16[104,1152]{1,0:T(8,128)(2,1)S(1)} collective-permute-done((bf16[104,1152]{1,0:T(8,128)(2,1)S(1)}, bf16[104,1152]{1,0:T(8,128)(2,1)S(1)}, u32[]{:S(2)}, u32[]{:S(2)}) %collective-permute-start.17) | collective-permute-done | bytes 239648 | tf_op jit(solution)/shard_map/ppermute | solution.py:288
  104.4 4.9 %collective-permute-done.8 = bf16[104,1280]{1,0:T(8,128)(2,1)S(1)} collective-permute-done((bf16[104,1280]{1,0:T(8,128)(2,1)S(1)}, bf16[104,1280]{1,0:T(8,128)(2,1)S(1)}, u32[]{:S(2)}, u32[]{:S(2)}) %collective-permute-start.8) | collective-permute-done | bytes 266272 | tf_op jit(solution)/shard_map/ppermute | solution.py:288
  110.4 1.6 collective-permute-start.31
  112.0 3.1 %collective-permute-done.9 = bf16[104,1280]{1,0:T(8,128)(2,1)S(1)} collective-permute-done((bf16[104,1280]{1,0:T(8,128)(2,1)S(1)}, bf16[104,1280]{1,0:T(8,128)(2,1)S(1)}, u32[]{:S(2)}, u32[]{:S(2)}) %collective-permute-start.9) | collective-permute-done | bytes 266272 | tf_op jit(solution)/shard_map/ppermute | solution.py:292
  115.4 1.6 collective-permute-start.26
  117.4 2.8 %collective-permute-start.22 = (bf16[72,1152]{1,0:T(8,128)(2,1)S(1)}, bf16[72,1152]{1,0:T(8,128)(2,1)S(1)}, u32[]{:S(2)}, u32[]{:S(2)}) collective-permute-start(bf16[72,1152]{1,0:T(8,128)(2,1)S(1)} %collective-permute-done.20.refs_3_), channel_id=1, source_target_pairs={{0,2},{1,3},{2,4},{3,5},{4,6},{5,7},{6,8},{7,9},{8,10},{9,11},{10,... | collective-permute-start | bytes 497672 | tf_op jit(solution)/shard_map/ppermute | solution.py:288
  120.2 2.4 %collective-permute-start.27 = (bf16[72,1280]{1,0:T(8,128)(2,1)S(1)}, bf16[72,1280]{1,0:T(8,128)(2,1)S(1)}, u32[]{:S(2)}, u32[]{:S(2)}) collective-permute-start(bf16[72,1280]{1,0:T(8,128)(2,1)S(1)} %collective-permute-done.26.refs_16_), channel_id=1, source_target_pairs={{0,14},{1,15},{2,0},{3,1},{4,2},{5,3},{6,4},{7,5},{8,6},{9,7},{10,... | collective-permute-start | bytes 552968 | tf_op jit(solution)/shard_map/ppermute | solution.py:288
  122.6 1.1 collective-permute-start.21
  124.4 1.9 collective-permute-start.24
  126.2 10.4 %collective-permute-start = (bf16[128,7168]{1,0:T(8,128)(2,1)S(1)}, bf16[128,7168]{1,0:T(8,128)(2,1)S(1)}, u32[]{:S(2)}, u32[]{:S(2)}) collective-permute-start(bf16[128,7168]{1,0:T(8,128)(2,1)S(1)} %bitcast.104), channel_id=1, source_target_pairs={{0,16},{16,32},{32,48},{48,64},{64,80},{80,96},{96,112},{112,128},... | collective-permute-start | bytes 5505032 | tf_op jit(solution)/shard_map/ppermute | solution.py:297
  136.6 3.0 %collective-permute-start.28 = (bf16[72,1280]{1,0:T(8,128)(2,1)S(1)}, bf16[72,1280]{1,0:T(8,128)(2,1)S(1)}, u32[]{:S(2)}, u32[]{:S(2)}) collective-permute-start(bf16[72,1280]{1,0:T(8,128)(2,1)S(1)} %collective-permute-done.27.refs_14_), channel_id=1, source_target_pairs={{0,14},{1,15},{2,0},{3,1},{4,2},{5,3},{6,4},{7,5},{8,6},{9,7},{10,... | collective-permute-start | bytes 552968 | tf_op jit(solution)/shard_map/ppermute | solution.py:288
  139.6 2.7 %collective-permute-start.33 = (bf16[72,1152]{1,0:T(8,128)(2,1)S(1)}, bf16[72,1152]{1,0:T(8,128)(2,1)S(1)}, u32[]{:S(2)}, u32[]{:S(2)}) collective-permute-start(bf16[72,1152]{1,0:T(8,128)(2,1)S(1)} %collective-permute-done.32.refs_15_), channel_id=1, source_target_pairs={{0,14},{1,15},{2,0},{3,1},{4,2},{5,3},{6,4},{7,5},{8,6},{9,7},{10,... | collective-permute-start | bytes 497672 | tf_op jit(solution)/shard_map/ppermute | solution.py:288
  142.3 1.8 collective-permute-start.30
  144.6 3.5 %collective-permute-start.29 = (bf16[40,1280]{1,0:T(8,128)(2,1)S(1)}, bf16[40,1280]{1,0:T(8,128)(2,1)S(1)}, u32[]{:S(2)}, u32[]{:S(2)}) collective-permute-start(bf16[40,1280]{1,0:T(8,128)(2,1)S(1)} %slice.181), channel_id=1, source_target_pairs={{0,14},{1,15},{2,0},{3,1},{4,2},{5,3},{6,4},{7,5},{8,6},{9,7},{10,... | collective-permute-start | bytes 307208 | tf_op jit(solution)/shard_map/ppermute | solution.py:288
  148.2 1.5 collective-permute-start.25
  149.8 2.1 %collective-permute-done.34.refs_11_ = bf16[40,1152]{1,0:T(8,128)(2,1)S(1)} collective-permute-done((bf16[40,1152]{1,0:T(8,128)(2,1)S(1)}, bf16[40,1152]{1,0:T(8,128)(2,1)S(1)}, u32[]{:S(2)}, u32[]{:S(2)}) %collective-permute-start.34) | collective-permute-done | bytes 92192 | tf_op jit(solution)/shard_map/ppermute | solution.py:288
  151.9 1.6 collective-permute-done.25.refs_8_
  153.5 5.6 %outward.1 = bf16[16,40,448]{2,1,0:T(8,128)(2,1)S(1)} custom-call(s32[1]{0:T(128)} %bitcast.1.node, bf16[448,2432]{1,0:T(8,128)(2,1)S(1)} %bitcast.101, bf16[2432,448]{1,0:T(8,128)(2,1)} %bitcast.99, bf16[72,1280]{1,0:T(8,128)(2,1)S(1)} %maximum_maximum_fusion.refs_0_, bf16[72,1152]{1,0:T(8,128)(2,1)S(1)} %maximum_maximum_fusion.1.refs_1_, ...), custom_call_target="tpu_custom_call" | custom-call | tf_op jit(solution)/shard_map/outward/pallas_call | solution.py:217
  159.1 21.9 %all_to_all.10.back = bf16[16,40,448]{2,1,0:T(8,128)(2,1)S(1)} all-to-all(bf16[16,40,448]{2,1,0:T(8,128)(2,1)S(1)} %outward.1), channel_id=1, replica_groups=mesh['section'=16,'expert'=16] {'expert'}, dimensions={0} | all-to-all | bytes 1146880 | tf_op jit(solution)/shard_map/all_to_all | solution.py:374
  181.0 2.1 %new_rows.1 = (bf16[24,7168]{1,0:T(8,128)(2,1)S(1)}, bf16[24,7168]{1,0:T(8,128)(2,1)S(1)}) custom-call(bf16[16,40,448]{2,1,0:T(8,128)(2,1)S(1)} %all_to_all.10.back, bf16[2,24,7168]{2,1,0:T(8,128)(2,1)S(1)} %copy-done.7, f32[24,128]{1,0:T(8,128)S(1)} %get-tuple-element.12.gate, f32[2,24,128]{2,1,0:T(8,128)S(1)} %get-tuple-element.13.meta), custom_call_target="tpu_custom_call" | custom-call | tf_op jit(solution)/shard_map/new_rows/pallas_call | solution.py:243
  183.2 10.3 %collective-permute-start.35 = (bf16[24,7168]{1,0:T(8,128)(2,1)S(1)}, bf16[24,7168]{1,0:T(8,128)(2,1)S(1)}, u32[]{:S(2)}, u32[]{:S(2)}) collective-permute-start(bf16[24,7168]{1,0:T(8,128)(2,1)S(1)} %get-tuple-element.14), channel_id=1, source_target_pairs={{0,16},{16,32},{32,48},{48,64},{64,80},{80,96},{96,112},{112,128},... | collective-permute-start | bytes 1032200 | tf_op jit(solution)/shard_map/ppermute | solution.py:297
  193.4 4.2 %collective-permute-done.35.frows.fhead = bf16[24,7168]{1,0:T(8,128)(2,1)S(1)} collective-permute-done((bf16[24,7168]{1,0:T(8,128)(2,1)S(1)}, bf16[24,7168]{1,0:T(8,128)(2,1)S(1)}, u32[]{:S(2)}, u32[]{:S(2)}) %collective-permute-start.35) | collective-permute-done | bytes 344096 | tf_op jit(solution)/shard_map/ppermute | solution.py:297
  197.6 2.8 %collective-permute-done.37.brows.bhead = bf16[24,7168]{1,0:T(8,128)(2,1)S(1)} collective-permute-done((bf16[24,7168]{1,0:T(8,128)(2,1)S(1)}, bf16[24,7168]{1,0:T(8,128)(2,1)S(1)}, u32[]{:S(2)}, u32[]{:S(2)}) %collective-permute-start.37) | collective-permute-done | bytes 344096 | tf_op jit(solution)/shard_map/ppermute | solution.py:297
  200.4 4.6 %patch.1 = (bf16[128,7168]{1,0:T(8,128)(2,1)}, bf16[128,7168]{1,0:T(8,128)(2,1)}) custom-call(bf16[128,7168]{1,0:T(8,128)(2,1)S(1)} %collective-permute-done.fraw, bf16[24,7168]{1,0:T(8,128)(2,1)S(1)} %collective-permute-done.35.frows.fhead, bf16[24,7168]{1,0:T(8,128)(2,1)S(1)} %collective-permute-done.35.frows.fhead, ...), custom_call_target="tpu_custom_call" | custom-call | tf_op jit(solution)/shard_map/patch/pallas_call | solution.py:275
  (93 shorter events, 15.2 us)
Async XLA Ops:
  3.8 1.5 copy-start.3
  5.3 1.5 copy-start.4
  14.9 33.0 %all-to-all-start = ((bf16[16,56,448]{2,1,0:T(8,128)(2,1)}), bf16[16,56,448]{2,1,0:T(8,128)(2,1)S(1)}, u32[]{:S(2)}, u32[]{:S(2)}) async-start(bf16[16,56,448]{2,1,0:T(8,128)(2,1)} %get-tuple-element.10), calls=%async_computation | async-start | bytes 1835008 | tf_op jit(solution)/shard_map/all_to_all | solution.py:361
  28.1 30.0 %copy-start = (bf16[1,2432,448]{2,1,0:T(8,128)(2,1)}, bf16[1,2432,448]{2,1,0:T(8,128)(2,1)S(1)}, u32[]{:S(2)}) copy-start(bf16[1,2432,448]{2,1,0:T(8,128)(2,1)S(1)} %copy.11) | copy-start | bytes 6537220
  47.9 1.6 copy-start.1
  58.1 18.4 %copy-start.8 = (bf16[8,104,2432]{2,1,0:T(8,128)(2,1)S(1)}, bf16[8,104,2432]{2,1,0:T(8,128)(2,1)}, u32[]{:S(2)}) copy-start(bf16[8,104,2432]{2,1,0:T(8,128)(2,1)} %partials.1) | copy-start | bytes 12140548
  61.4 5.3 %collective-permute-start.10 = (bf16[48,1152]{1,0:T(8,128)(2,1)S(1)}, bf16[48,1152]{1,0:T(8,128)(2,1)S(1)}, u32[]{:S(2)}, u32[]{:S(2)}) collective-permute-start(bf16[48,1152]{1,0:T(8,128)(2,1)S(1)} %get-tuple-element.20), channel_id=1, source_target_pairs={{0,2},{1,3},{2,4},{3,5},{4,6},{5,7},{6,8},{7,9},{8,10},{9,11},{10,... | collective-permute-start | bytes 331784 | tf_op jit(solution)/shard_map/ppermute | solution.py:288
  63.2 9.6 %collective-permute-start.14 = (bf16[56,1152]{1,0:T(8,128)(2,1)S(1)}, bf16[56,1152]{1,0:T(8,128)(2,1)S(1)}, u32[]{:S(2)}, u32[]{:S(2)}) collective-permute-start(bf16[56,1152]{1,0:T(8,128)(2,1)S(1)} %get-tuple-element.23), channel_id=1, source_target_pairs={{0,14},{1,15},{2,0},{3,1},{4,2},{5,3},{6,4},{7,5},{8,6},{9,7},{10,... | collective-permute-start | bytes 387080 | tf_op jit(solution)/shard_map/ppermute | solution.py:288
  65.2 11.3 %collective-permute-start.5 = (bf16[56,1280]{1,0:T(8,128)(2,1)S(1)}, bf16[56,1280]{1,0:T(8,128)(2,1)S(1)}, u32[]{:S(2)}, u32[]{:S(2)}) collective-permute-start(bf16[56,1280]{1,0:T(8,128)(2,1)S(1)} %get-tuple-element.29), channel_id=1, source_target_pairs={{0,14},{1,15},{2,0},{3,1},{4,2},{5,3},{6,4},{7,5},{8,6},{9,7},{10,... | collective-permute-start | bytes 430088 | tf_op jit(solution)/shard_map/ppermute | solution.py:288
  65.7 6.0 %collective-permute-start.1 = (bf16[48,1280]{1,0:T(8,128)(2,1)S(1)}, bf16[48,1280]{1,0:T(8,128)(2,1)S(1)}, u32[]{:S(2)}, u32[]{:S(2)}) collective-permute-start(bf16[48,1280]{1,0:T(8,128)(2,1)S(1)} %get-tuple-element.26), channel_id=1, source_target_pairs={{0,2},{1,3},{2,4},{3,5},{4,6},{5,7},{6,8},{7,9},{8,10},{9,11},{10,... | collective-permute-start | bytes 368648 | tf_op jit(solution)/shard_map/ppermute | solution.py:288
  67.7 9.0 %collective-permute-start.11 = (bf16[104,1152]{1,0:T(8,128)(2,1)S(1)}, bf16[104,1152]{1,0:T(8,128)(2,1)S(1)}, u32[]{:S(2)}, u32[]{:S(2)}) collective-permute-start(bf16[104,1152]{1,0:T(8,128)(2,1)S(1)} %pad_maximum_fusion.2), channel_id=1, source_target_pairs={{0,2},{1,3},{2,4},{3,5},{4,6},{5,7},{6,8},{7,9},{8,10},{9,11},{10,... | collective-permute-start | bytes 718856 | tf_op jit(solution)/shard_map/ppermute | solution.py:288
  72.7 8.9 %collective-permute-start.2 = (bf16[104,1280]{1,0:T(8,128)(2,1)S(1)}, bf16[104,1280]{1,0:T(8,128)(2,1)S(1)}, u32[]{:S(2)}, u32[]{:S(2)}) collective-permute-start(bf16[104,1280]{1,0:T(8,128)(2,1)S(1)} %pad_maximum_fusion), channel_id=1, source_target_pairs={{0,2},{1,3},{2,4},{3,5},{4,6},{5,7},{6,8},{7,9},{8,10},{9,11},{10,... | collective-permute-start | bytes 798728 | tf_op jit(solution)/shard_map/ppermute | solution.py:288
  73.8 8.0 %collective-permute-start.15 = (bf16[104,1152]{1,0:T(8,128)(2,1)S(1)}, bf16[104,1152]{1,0:T(8,128)(2,1)S(1)}, u32[]{:S(2)}, u32[]{:S(2)}) collective-permute-start(bf16[104,1152]{1,0:T(8,128)(2,1)S(1)} %pad_maximum_fusion.3), channel_id=1, source_target_pairs={{0,14},{1,15},{2,0},{3,1},{4,2},{5,3},{6,4},{7,5},{8,6},{9,7},{10,... | collective-permute-start | bytes 718856 | tf_op jit(solution)/shard_map/ppermute | solution.py:288
  76.6 11.8 %collective-permute-start.6 = (bf16[104,1280]{1,0:T(8,128)(2,1)S(1)}, bf16[104,1280]{1,0:T(8,128)(2,1)S(1)}, u32[]{:S(2)}, u32[]{:S(2)}) collective-permute-start(bf16[104,1280]{1,0:T(8,128)(2,1)S(1)} %pad_maximum_fusion.1), channel_id=1, source_target_pairs={{0,14},{1,15},{2,0},{3,1},{4,2},{5,3},{6,4},{7,5},{8,6},{9,7},{10,... | collective-permute-start | bytes 798728 | tf_op jit(solution)/shard_map/ppermute | solution.py:288
  76.8 9.9 %collective-permute-start.12 = (bf16[104,1152]{1,0:T(8,128)(2,1)S(1)}, bf16[104,1152]{1,0:T(8,128)(2,1)S(1)}, u32[]{:S(2)}, u32[]{:S(2)}) collective-permute-start(bf16[104,1152]{1,0:T(8,128)(2,1)S(1)} %fusion.8), channel_id=1, source_target_pairs={{0,2},{1,3},{2,4},{3,5},{4,6},{5,7},{6,8},{7,9},{8,10},{9,11},{10,... | collective-permute-start | bytes 718856 | tf_op jit(solution)/shard_map/ppermute | solution.py:288
  81.6 10.8 %collective-permute-start.3 = (bf16[104,1280]{1,0:T(8,128)(2,1)S(1)}, bf16[104,1280]{1,0:T(8,128)(2,1)S(1)}, u32[]{:S(2)}, u32[]{:S(2)}) collective-permute-start(bf16[104,1280]{1,0:T(8,128)(2,1)S(1)} %fusion.2), channel_id=1, source_target_pairs={{0,2},{1,3},{2,4},{3,5},{4,6},{5,7},{6,8},{7,9},{8,10},{9,11},{10,... | collective-permute-start | bytes 798728 | tf_op jit(solution)/shard_map/ppermute | solution.py:288
  86.8 7.3 %collective-permute-start.16 = (bf16[104,1152]{1,0:T(8,128)(2,1)S(1)}, bf16[104,1152]{1,0:T(8,128)(2,1)S(1)}, u32[]{:S(2)}, u32[]{:S(2)}) collective-permute-start(bf16[104,1152]{1,0:T(8,128)(2,1)S(1)} %get-tuple-element.19), channel_id=1, source_target_pairs={{0,14},{1,15},{2,0},{3,1},{4,2},{5,3},{6,4},{7,5},{8,6},{9,7},{10,... | collective-permute-start | bytes 718856 | tf_op jit(solution)/shard_map/ppermute | solution.py:288
  86.9 13.8 %collective-permute-start.13 = (bf16[104,1152]{1,0:T(8,128)(2,1)S(1)}, bf16[104,1152]{1,0:T(8,128)(2,1)S(1)}, u32[]{:S(2)}, u32[]{:S(2)}) collective-permute-start(bf16[104,1152]{1,0:T(8,128)(2,1)S(1)} %get-tuple-element.18), channel_id=1, source_target_pairs={{0,2},{1,3},{2,4},{3,5},{4,6},{5,7},{6,8},{7,9},{8,10},{9,11},{10,... | collective-permute-start | bytes 718856 | tf_op jit(solution)/shard_map/ppermute | solution.py:288
  92.5 33.7 %copy-start.5 = (bf16[1,128,7168]{2,1,0:T(8,128)(2,1)S(1)}, bf16[1,128,7168]{2,1,0:T(8,128)(2,1)}, u32[]{:S(2)}) copy-start(bf16[1,128,7168]{2,1,0:T(8,128)(2,1)} %param.9) | copy-start | bytes 5505028
  92.6 44.0 %copy-start.9 = (bf16[1,128,7168]{2,1,0:T(8,128)(2,1)S(1)}, bf16[1,128,7168]{2,1,0:T(8,128)(2,1)}, u32[]{:S(2)}) copy-start(bf16[1,128,7168]{2,1,0:T(8,128)(2,1)} %param.11) | copy-start | bytes 5505028
  92.6 6.5 %collective-permute-start.7 = (bf16[104,1280]{1,0:T(8,128)(2,1)S(1)}, bf16[104,1280]{1,0:T(8,128)(2,1)S(1)}, u32[]{:S(2)}, u32[]{:S(2)}) collective-permute-start(bf16[104,1280]{1,0:T(8,128)(2,1)S(1)} %get-tuple-element.25), channel_id=1, source_target_pairs={{0,14},{1,15},{2,0},{3,1},{4,2},{5,3},{6,4},{7,5},{8,6},{9,7},{10,... | collective-permute-start | bytes 798728 | tf_op jit(solution)/shard_map/ppermute | solution.py:288
  92.7 11.8 %collective-permute-start.4 = (bf16[104,1280]{1,0:T(8,128)(2,1)S(1)}, bf16[104,1280]{1,0:T(8,128)(2,1)S(1)}, u32[]{:S(2)}, u32[]{:S(2)}) collective-permute-start(bf16[104,1280]{1,0:T(8,128)(2,1)S(1)} %get-tuple-element.24), channel_id=1, source_target_pairs={{0,2},{1,3},{2,4},{3,5},{4,6},{5,7},{6,8},{7,9},{8,10},{9,11},{10,... | collective-permute-start | bytes 798728 | tf_op jit(solution)/shard_map/ppermute | solution.py:288
  94.2 59.3 %copy-start.2 = (bf16[1,448,2432]{2,1,0:T(8,128)(2,1)S(1)}, bf16[1,448,2432]{2,1,0:T(8,128)(2,1)}, u32[]{:S(2)}) copy-start(bf16[1,448,2432]{2,1,0:T(8,128)(2,1)} %param.16) | copy-start | bytes 6537220
  94.2 9.4 %collective-permute-start.17 = (bf16[104,1152]{1,0:T(8,128)(2,1)S(1)}, bf16[104,1152]{1,0:T(8,128)(2,1)S(1)}, u32[]{:S(2)}, u32[]{:S(2)}) collective-permute-start(bf16[104,1152]{1,0:T(8,128)(2,1)S(1)} %fusion.7), channel_id=1, source_target_pairs={{0,14},{1,15},{2,0},{3,1},{4,2},{5,3},{6,4},{7,5},{8,6},{9,7},{10,... | collective-permute-start | bytes 718856 | tf_op jit(solution)/shard_map/ppermute | solution.py:288
  99.2 10.2 %collective-permute-start.8 = (bf16[104,1280]{1,0:T(8,128)(2,1)S(1)}, bf16[104,1280]{1,0:T(8,128)(2,1)S(1)}, u32[]{:S(2)}, u32[]{:S(2)}) collective-permute-start(bf16[104,1280]{1,0:T(8,128)(2,1)S(1)} %fusion.1), channel_id=1, source_target_pairs={{0,14},{1,15},{2,0},{3,1},{4,2},{5,3},{6,4},{7,5},{8,6},{9,7},{10,... | collective-permute-start | bytes 798728 | tf_op jit(solution)/shard_map/ppermute | solution.py:288
  103.7 6.4 %collective-permute-start.18 = (bf16[104,1152]{1,0:T(8,128)(2,1)S(1)}, bf16[104,1152]{1,0:T(8,128)(2,1)S(1)}, u32[]{:S(2)}, u32[]{:S(2)}) collective-permute-start(bf16[104,1152]{1,0:T(8,128)(2,1)S(1)} %fusion.11), channel_id=1, source_target_pairs={{0,1},{1,0},{2,3},{3,2},{4,5},{5,4},{6,7},{7,6},{8,9},{9,8},{10,11... | collective-permute-start | bytes 718856 | tf_op jit(solution)/shard_map/ppermute | solution.py:292
  109.5 5.6 %collective-permute-start.9 = (bf16[104,1280]{1,0:T(8,128)(2,1)S(1)}, bf16[104,1280]{1,0:T(8,128)(2,1)S(1)}, u32[]{:S(2)}, u32[]{:S(2)}) collective-permute-start(bf16[104,1280]{1,0:T(8,128)(2,1)S(1)} %fusion.5), channel_id=1, source_target_pairs={{0,1},{1,0},{2,3},{3,2},{4,5},{5,4},{6,7},{7,6},{8,9},{9,8},{10,11... | collective-permute-start | bytes 798728 | tf_op jit(solution)/shard_map/ppermute | solution.py:292
  110.4 9.8 %collective-permute-start.31 = (bf16[72,1152]{1,0:T(8,128)(2,1)S(1)}, bf16[72,1152]{1,0:T(8,128)(2,1)S(1)}, u32[]{:S(2)}, u32[]{:S(2)}) collective-permute-start(bf16[72,1152]{1,0:T(8,128)(2,1)S(1)} %maximum_maximum_fusion.1.refs_1_), channel_id=1, source_target_pairs={{0,14},{1,15},{2,0},{3,1},{4,2},{5,3},{6,4},{7,5},{8,6},{9,7},{10,... | collective-permute-start | bytes 497672 | tf_op jit(solution)/shard_map/ppermute | solution.py:288
  112.0 5.4 %collective-permute-start.20 = (bf16[72,1152]{1,0:T(8,128)(2,1)S(1)}, bf16[72,1152]{1,0:T(8,128)(2,1)S(1)}, u32[]{:S(2)}, u32[]{:S(2)}) collective-permute-start(bf16[72,1152]{1,0:T(8,128)(2,1)S(1)} %maximum_maximum_fusion.1.refs_1_), channel_id=1, source_target_pairs={{0,2},{1,3},{2,4},{3,5},{4,6},{5,7},{6,8},{7,9},{8,10},{9,11},{10,... | collective-permute-start | bytes 497672 | tf_op jit(solution)/shard_map/ppermute | solution.py:288
  115.4 4.8 %collective-permute-start.26 = (bf16[72,1280]{1,0:T(8,128)(2,1)S(1)}, bf16[72,1280]{1,0:T(8,128)(2,1)S(1)}, u32[]{:S(2)}, u32[]{:S(2)}) collective-permute-start(bf16[72,1280]{1,0:T(8,128)(2,1)S(1)} %maximum_maximum_fusion.refs_0_), channel_id=1, source_target_pairs={{0,14},{1,15},{2,0},{3,1},{4,2},{5,3},{6,4},{7,5},{8,6},{9,7},{10,... | collective-permute-start | bytes 552968 | tf_op jit(solution)/shard_map/ppermute | solution.py:288
  117.0 5.6 %collective-permute-start.19 = (bf16[72,1280]{1,0:T(8,128)(2,1)S(1)}, bf16[72,1280]{1,0:T(8,128)(2,1)S(1)}, u32[]{:S(2)}, u32[]{:S(2)}) collective-permute-start(bf16[72,1280]{1,0:T(8,128)(2,1)S(1)} %maximum_maximum_fusion.refs_0_), channel_id=1, source_target_pairs={{0,2},{1,3},{2,4},{3,5},{4,6},{5,7},{6,8},{7,9},{8,10},{9,11},{10,... | collective-permute-start | bytes 552968 | tf_op jit(solution)/shard_map/ppermute | solution.py:288
  117.4 6.9 %collective-permute-start.22 = (bf16[72,1152]{1,0:T(8,128)(2,1)S(1)}, bf16[72,1152]{1,0:T(8,128)(2,1)S(1)}, u32[]{:S(2)}, u32[]{:S(2)}) collective-permute-start(bf16[72,1152]{1,0:T(8,128)(2,1)S(1)} %collective-permute-done.20.refs_3_), channel_id=1, source_target_pairs={{0,2},{1,3},{2,4},{3,5},{4,6},{5,7},{6,8},{7,9},{8,10},{9,11},{10,... | collective-permute-start | bytes 497672 | tf_op jit(solution)/shard_map/ppermute | solution.py:288
  120.2 16.4 %collective-permute-start.32 = (bf16[72,1152]{1,0:T(8,128)(2,1)S(1)}, bf16[72,1152]{1,0:T(8,128)(2,1)S(1)}, u32[]{:S(2)}, u32[]{:S(2)}) collective-permute-start(bf16[72,1152]{1,0:T(8,128)(2,1)S(1)} %collective-permute-done.31.refs_17_), channel_id=1, source_target_pairs={{0,14},{1,15},{2,0},{3,1},{4,2},{5,3},{6,4},{7,5},{8,6},{9,7},{10,... | collective-permute-start | bytes 497672 | tf_op jit(solution)/shard_map/ppermute | solution.py:288
  120.2 16.4 %collective-permute-start.27 = (bf16[72,1280]{1,0:T(8,128)(2,1)S(1)}, bf16[72,1280]{1,0:T(8,128)(2,1)S(1)}, u32[]{:S(2)}, u32[]{:S(2)}) collective-permute-start(bf16[72,1280]{1,0:T(8,128)(2,1)S(1)} %collective-permute-done.26.refs_16_), channel_id=1, source_target_pairs={{0,14},{1,15},{2,0},{3,1},{4,2},{5,3},{6,4},{7,5},{8,6},{9,7},{10,... | collective-permute-start | bytes 552968 | tf_op jit(solution)/shard_map/ppermute | solution.py:288
  122.6 17.0 %collective-permute-start.21 = (bf16[72,1280]{1,0:T(8,128)(2,1)S(1)}, bf16[72,1280]{1,0:T(8,128)(2,1)S(1)}, u32[]{:S(2)}, u32[]{:S(2)}) collective-permute-start(bf16[72,1280]{1,0:T(8,128)(2,1)S(1)} %collective-permute-done.19.refs_2_), channel_id=1, source_target_pairs={{0,2},{1,3},{2,4},{3,5},{4,6},{5,7},{6,8},{7,9},{8,10},{9,11},{10,... | collective-permute-start | bytes 552968 | tf_op jit(solution)/shard_map/ppermute | solution.py:288
  124.4 15.3 %collective-permute-start.24 = (bf16[72,1152]{1,0:T(8,128)(2,1)S(1)}, bf16[72,1152]{1,0:T(8,128)(2,1)S(1)}, u32[]{:S(2)}, u32[]{:S(2)}) collective-permute-start(bf16[72,1152]{1,0:T(8,128)(2,1)S(1)} %collective-permute-done.22.refs_5_), channel_id=1, source_target_pairs={{0,2},{1,3},{2,4},{3,5},{4,6},{5,7},{6,8},{7,9},{8,10},{9,11},{10,... | collective-permute-start | bytes 497672 | tf_op jit(solution)/shard_map/ppermute | solution.py:288
  126.2 67.2 %collective-permute-start = (bf16[128,7168]{1,0:T(8,128)(2,1)S(1)}, bf16[128,7168]{1,0:T(8,128)(2,1)S(1)}, u32[]{:S(2)}, u32[]{:S(2)}) collective-permute-start(bf16[128,7168]{1,0:T(8,128)(2,1)S(1)} %bitcast.104), channel_id=1, source_target_pairs={{0,16},{16,32},{32,48},{48,64},{64,80},{80,96},{96,112},{112,128},... | collective-permute-start | bytes 5505032 | tf_op jit(solution)/shard_map/ppermute | solution.py:297
  136.6 56.8 %collective-permute-start.36 = (bf16[128,7168]{1,0:T(8,128)(2,1)S(1)}, bf16[128,7168]{1,0:T(8,128)(2,1)S(1)}, u32[]{:S(2)}, u32[]{:S(2)}) collective-permute-start(bf16[128,7168]{1,0:T(8,128)(2,1)S(1)} %bitcast.110), channel_id=1, source_target_pairs={{0,240},{16,0},{32,16},{48,32},{64,48},{80,64},{96,80},{112,96},{1... | collective-permute-start | bytes 5505032 | tf_op jit(solution)/shard_map/ppermute | solution.py:297
  136.6 5.7 %collective-permute-start.28 = (bf16[72,1280]{1,0:T(8,128)(2,1)S(1)}, bf16[72,1280]{1,0:T(8,128)(2,1)S(1)}, u32[]{:S(2)}, u32[]{:S(2)}) collective-permute-start(bf16[72,1280]{1,0:T(8,128)(2,1)S(1)} %collective-permute-done.27.refs_14_), channel_id=1, source_target_pairs={{0,14},{1,15},{2,0},{3,1},{4,2},{5,3},{6,4},{7,5},{8,6},{9,7},{10,... | collective-permute-start | bytes 552968 | tf_op jit(solution)/shard_map/ppermute | solution.py:288
  139.6 8.4 %collective-permute-start.23 = (bf16[72,1280]{1,0:T(8,128)(2,1)S(1)}, bf16[72,1280]{1,0:T(8,128)(2,1)S(1)}, u32[]{:S(2)}, u32[]{:S(2)}) collective-permute-start(bf16[72,1280]{1,0:T(8,128)(2,1)S(1)} %collective-permute-done.21.refs_4_), channel_id=1, source_target_pairs={{0,2},{1,3},{2,4},{3,5},{4,6},{5,7},{6,8},{7,9},{8,10},{9,11},{10,... | collective-permute-start | bytes 552968 | tf_op jit(solution)/shard_map/ppermute | solution.py:288
  139.6 5.0 %collective-permute-start.33 = (bf16[72,1152]{1,0:T(8,128)(2,1)S(1)}, bf16[72,1152]{1,0:T(8,128)(2,1)S(1)}, u32[]{:S(2)}, u32[]{:S(2)}) collective-permute-start(bf16[72,1152]{1,0:T(8,128)(2,1)S(1)} %collective-permute-done.32.refs_15_), channel_id=1, source_target_pairs={{0,14},{1,15},{2,0},{3,1},{4,2},{5,3},{6,4},{7,5},{8,6},{9,7},{10,... | collective-permute-start | bytes 497672 | tf_op jit(solution)/shard_map/ppermute | solution.py:288
  142.3 5.9 %collective-permute-start.30 = (bf16[32,1152]{1,0:T(8,128)(2,1)S(1)}, bf16[32,1152]{1,0:T(8,128)(2,1)S(1)}, u32[]{:S(2)}, u32[]{:S(2)}) collective-permute-start(bf16[32,1152]{1,0:T(8,128)(2,1)S(1)} %slice.182), channel_id=1, source_target_pairs={{0,2},{1,3},{2,4},{3,5},{4,6},{5,7},{6,8},{7,9},{8,10},{9,11},{10,... | collective-permute-start | bytes 221192 | tf_op jit(solution)/shard_map/ppermute | solution.py:288
  144.6 8.9 %collective-permute-start.29 = (bf16[40,1280]{1,0:T(8,128)(2,1)S(1)}, bf16[40,1280]{1,0:T(8,128)(2,1)S(1)}, u32[]{:S(2)}, u32[]{:S(2)}) collective-permute-start(bf16[40,1280]{1,0:T(8,128)(2,1)S(1)} %slice.181), channel_id=1, source_target_pairs={{0,14},{1,15},{2,0},{3,1},{4,2},{5,3},{6,4},{7,5},{8,6},{9,7},{10,... | collective-permute-start | bytes 307208 | tf_op jit(solution)/shard_map/ppermute | solution.py:288
  148.1 3.8 %collective-permute-start.34 = (bf16[40,1152]{1,0:T(8,128)(2,1)S(1)}, bf16[40,1152]{1,0:T(8,128)(2,1)S(1)}, u32[]{:S(2)}, u32[]{:S(2)}) collective-permute-start(bf16[40,1152]{1,0:T(8,128)(2,1)S(1)} %slice.183), channel_id=1, source_target_pairs={{0,14},{1,15},{2,0},{3,1},{4,2},{5,3},{6,4},{7,5},{8,6},{9,7},{10,... | collective-permute-start | bytes 276488 | tf_op jit(solution)/shard_map/ppermute | solution.py:288
  148.2 32.8 %copy-start.7 = (bf16[2,24,7168]{2,1,0:T(8,128)(2,1)S(1)}, bf16[2,24,7168]{2,1,0:T(8,128)(2,1)}, u32[]{:S(2)}) copy-start(bf16[2,24,7168]{2,1,0:T(8,128)(2,1)} %copy-done.6) | copy-start | bytes 2064388
  148.2 5.3 %collective-permute-start.25 = (bf16[32,1280]{1,0:T(8,128)(2,1)S(1)}, bf16[32,1280]{1,0:T(8,128)(2,1)S(1)}, u32[]{:S(2)}, u32[]{:S(2)}) collective-permute-start(bf16[32,1280]{1,0:T(8,128)(2,1)S(1)} %slice.180), channel_id=1, source_target_pairs={{0,2},{1,3},{2,4},{3,5},{4,6},{5,7},{6,8},{7,9},{8,10},{9,11},{10,... | collective-permute-start | bytes 245768 | tf_op jit(solution)/shard_map/ppermute | solution.py:288
  183.2 14.5 %collective-permute-start.35 = (bf16[24,7168]{1,0:T(8,128)(2,1)S(1)}, bf16[24,7168]{1,0:T(8,128)(2,1)S(1)}, u32[]{:S(2)}, u32[]{:S(2)}) collective-permute-start(bf16[24,7168]{1,0:T(8,128)(2,1)S(1)} %get-tuple-element.14), channel_id=1, source_target_pairs={{0,16},{16,32},{32,48},{48,64},{64,80},{80,96},{96,112},{112,128},... | collective-permute-start | bytes 1032200 | tf_op jit(solution)/shard_map/ppermute | solution.py:297
  193.4 7.0 %collective-permute-start.37 = (bf16[24,7168]{1,0:T(8,128)(2,1)S(1)}, bf16[24,7168]{1,0:T(8,128)(2,1)S(1)}, u32[]{:S(2)}, u32[]{:S(2)}) collective-permute-start(bf16[24,7168]{1,0:T(8,128)(2,1)S(1)} %get-tuple-element.15), channel_id=1, source_target_pairs={{0,240},{16,0},{32,16},{48,32},{64,48},{80,64},{96,80},{112,96},{1... | collective-permute-start | bytes 1032200 | tf_op jit(solution)/shard_map/ppermute | solution.py:297
  (1 other events, 0.8 us)
